TPU v7x, 512 devices: a whole 4x4x16 slice. The times are simulated.
512 devices in a mesh: tile: 32 (over x, z_hi, core), dir: 16 (over y, z_lo).
Axes of the slice: x: 4, y: 4, z: 16 (z_hi: 4, z_lo: 4; z = z_hi * 4 + z_lo), core: 2. Of those that a mesh axis runs over, the one named last changes fastest.
Arguments:
- background_prev: float32 [64, 256, 128], P(None, 'tile'), may hold values from -6 to 6
- background_now: float32 [64, 256, 128], P(None, 'tile'), may hold values from -6 to 6
- stiffness: bfloat16 [64, 256, 128], P(None, 'tile'), may hold values from 0.039794922 to 0.19921875
- drift_terms: bfloat16 [3, 64, 256, 128], P(None, None, 'tile'), may hold values from -0.079589844 to 0.079589844
- born_prev: bfloat16 [64, 64, 256, 128], P('dir', None, 'tile'), may hold values from -6 to 6
- born_now: bfloat16 [64, 64, 256, 128], P('dir', None, 'tile'), may hold values from -6 to 6
- pieces: bfloat16 [64, 1024, 32, 128], P('dir', 'tile'), may hold values from -6 to 6
- piece_target: int32 [1024, 1], P('tile'), may hold values from 0 to 31; in each aligned block of 32 rows (0 to 31, 32 to 63, ...) at most 2 rows name the same one
- piece_block: int32 [1024], P('tile'), may hold values from 0 to 15
- wavelet: float32 [4], replicated, may hold values from -24 to 24
- source_cell: int32 [3], replicated, may hold values from 0 to 63
- receiver_z: int32 [256], replicated, may hold values from 0 to 63
- receiver_x: int32 [256], replicated, may hold values from 0 to 255
- receiver_y: int32 [256], replicated, may hold values from 0 to 127
Outputs:
- born_field: float32 [64, 64, 256, 128], P('dir', None, 'tile')
- traces: float32 [64, 4, 256], P('dir')
Inputs may be any that keep to these rules, and one draw needn't show every extreme that they name: `piece_target`: in each aligned block of 32 rows (the rows of one device) no tile is named by more than 2 rows; in some blocks a tile is named by exactly 2 rows.
All inputs are finite; a program needn't handle non-finite values.
Results may differ from a plain program's by a relative error of at most 0.0005.
Values may be sent and summed in bfloat16 or wider, within the bound.
No kernel may reach another device: no remote copies, remote signals or barrier semaphores. Data moves between devices by JAX's collectives and lax.ppermute only.
A program may use at most 128 MiB of HBM per device.

v0:
```python
import jax
import jax.numpy as jnp
from jax import lax
from jax.sharding import PartitionSpec as P

CX = 8
ITERS = 4
ZPARTS = 2
CAP = 2
SECOND_TAPS = (-205.0 / 72.0, 8.0 / 5.0, -1.0 / 5.0, 8.0 / 315.0, -1.0 / 560.0)
FIRST_TAPS = (0.0, 4.0 / 5.0, -1.0 / 5.0, 4.0 / 105.0, -1.0 / 280.0)


def padded_2(block, sides, width):
    for axis, dim in sides:
        count = lax.axis_size(axis)
        forward = [(i, i + 1) for i in range(count - 1)]
        backward = [(target, source) for source, target in forward]
        low = lax.ppermute(
            lax.slice_in_dim(block, block.shape[dim] - width, None, axis=dim), axis, forward
        )
        high = lax.ppermute(lax.slice_in_dim(block, 0, width, axis=dim), axis, backward)
        block = jnp.concatenate([low, block, high], axis=dim)
    return block


def shifted(padded, interior, spatial, offset):
    starts = [4, 4, 4]
    starts[spatial] = 4 + offset
    leading = padded.ndim - 3
    window = tuple(
        [slice(None)] * leading
        + [slice(starts[which], starts[which] + interior[which]) for which in range(3)]
    )
    return padded[window]


def operate(padded, stiff_wide, drift_wide):
    interior = stiff_wide.shape
    center = shifted(padded, interior, 0, 0)
    second = 3.0 * SECOND_TAPS[0] * center
    slopes = jnp.zeros_like(center)
    for spatial in range(3):
        gradient = jnp.zeros_like(center)
        for offset in range(1, 5):
            forward = shifted(padded, interior, spatial, offset)
            backward = shifted(padded, interior, spatial, -offset)
            second = second + SECOND_TAPS[offset] * (forward + backward)
            gradient = gradient + FIRST_TAPS[offset] * (forward - backward)
        slopes = slopes + drift_wide[spatial] * gradient
    return stiff_wide * second + slopes


def faces(born_present, background_part):
    return (padded_2(born_present, (("tile", 2),), 4), padded_2(background_part, (("tile", 2),), 4))


def assemble(pieces, piece_target, piece_block, tile_count):
    targets = piece_target[:, 0]
    row_count = targets.shape[0]
    positions = jnp.arange(row_count)
    before = (targets[:, None] == targets[None, :]) & (positions[None, :] < positions[:, None])
    arrival = jnp.sum(before.astype(jnp.int32), axis=1)
    slot_ids = targets * CAP + arrival
    placing = (slot_ids[:, None] == jnp.arange(tile_count * CAP)[None, :]).astype(jnp.bfloat16)
    outgoing = jnp.einsum(
        "krzy,rs->kszy", pieces, placing, preferred_element_type=jnp.float32
    ).astype(jnp.bfloat16)
    labels = jnp.dot(
        (piece_block + 1).astype(jnp.bfloat16)[None, :], placing, preferred_element_type=jnp.float32
    ).astype(jnp.bfloat16)
    incoming, arrived = (
        lax.all_to_all(outgoing, "tile", split_axis=1, concat_axis=1, tiled=True),
        lax.all_to_all(labels, "tile", split_axis=1, concat_axis=1, tiled=True),
    )
    wanted = (jnp.arange(ZPARTS * CX) + 1).astype(jnp.float32)
    picking = (
        (arrived[0][:, None].astype(jnp.float32) == wanted[None, :])
        .astype(jnp.bfloat16)
        .reshape(-1, ZPARTS, CX)
    )
    perturb = jnp.einsum("kszy,spx->kpzxy", incoming, picking, preferred_element_type=jnp.float32)
    return perturb.reshape(pieces.shape[0], ZPARTS * pieces.shape[2], CX, pieces.shape[3])


def local(
    background_prev,
    background_now,
    stiffness,
    drift_terms,
    born_prev,
    born_now,
    pieces,
    piece_target,
    piece_block,
    wavelet,
    source_cell,
    receiver_z,
    receiver_x,
    receiver_y,
):
    tile_count = lax.axis_size("tile")
    tile_place = lax.axis_index("tile")
    depth_cells, width_cells, height_cells = background_now.shape
    stiff_wide = stiffness.astype(jnp.float32)
    drift_wide = drift_terms.astype(jnp.float32)
    perturb = assemble(pieces, piece_target, piece_block, tile_count)
    across_axis = (tile_place * width_cells + jnp.arange(width_cells))[None, :, None]
    height_axis = jnp.arange(height_cells)[None, None, :]
    earlier_born = born_prev.astype(jnp.float32)
    current_born = born_now.astype(jnp.float32)
    local_x = receiver_x - tile_place * width_cells
    inside = ((local_x >= 0) & (local_x < width_cells)).astype(jnp.float32)
    flat_index = (
        receiver_z * width_cells + jnp.clip(local_x, 0, width_cells - 1)
    ) * height_cells + receiver_y
    slab_cells = depth_cells // lax.axis_size("dir")
    slab_start = lax.axis_index("dir") * slab_cells
    previous = lax.dynamic_slice_in_dim(background_prev, slab_start, slab_cells, 0)
    present = lax.dynamic_slice_in_dim(background_now, slab_start, slab_cells, 0)
    slab_stiff = lax.dynamic_slice_in_dim(stiff_wide, slab_start, slab_cells, 0)
    slab_drift = lax.dynamic_slice_in_dim(drift_wide, slab_start, slab_cells, 1)
    depth_axis = (slab_start + jnp.arange(slab_cells))[:, None, None]
    source_mask = (
        (depth_axis == source_cell[0])
        & (across_axis == source_cell[1])
        & (height_axis == source_cell[2])
    ).astype(jnp.float32)
    records = []
    for step_index in range(ITERS):
        deeper = padded_2(present[None], (("dir", 1),), 4)
        born_wide, back_wide = faces(current_born, deeper)
        local_accel = operate(
            jnp.pad(back_wide[0], ((0, 0), (0, 0), (4, 4))), slab_stiff, slab_drift
        )
        acceleration = lax.all_gather(local_accel, "dir", axis=0, tiled=True)
        previous, present = (
            present,
            2.0 * present - previous + local_accel + wavelet[step_index] * source_mask,
        )
        born_padded = jnp.pad(born_wide, ((0, 0), (4, 4), (0, 0), (4, 4)))
        following = (
            2.0 * current_born
            - earlier_born
            + operate(born_padded, stiff_wide, drift_wide)
            + perturb * acceleration
        )
        records.append(
            jnp.take(following.reshape(following.shape[0], -1), flat_index, axis=1)
            * inside[None, :]
        )
        earlier_born, current_born = (current_born, following)
    traces = lax.psum(jnp.stack(records, axis=1), "tile")
    return (current_born, traces)


def solution(mesh):
    placed = (
        P(None, "tile", None),
        P(None, "tile", None),
        P(None, "tile", None),
        P(None, None, "tile", None),
        P("dir", None, "tile", None),
        P("dir", None, "tile", None),
        P("dir", "tile", None, None),
        P("tile", None),
        P("tile"),
        P(),
        P(),
        P(),
        P(),
        P(),
    )
    return jax.shard_map(
        local,
        mesh=mesh,
        in_specs=placed,
        out_specs=(P("dir", None, "tile", None), P("dir", None, None)),
        check_vma=False,
    )
```

profile of v0, /device:TPU:24, one launch (start us, length us, event | category | flops | bytes accessed | tf_op | source)
XLA Modules:
  0.0 746.2 jit_solution(9172707135732427772)
XLA Ops:
  0.6 0.9 convert_reduce_fusion.1
  2.2 0.8 fusion.9
  3.8 17.9 %all-to-all-start = ((bf16[1,32,2]{2,0,1:T(2,128)(2,1)}), bf16[1,32,2]{2,0,1:T(2,128)(2,1)S(1)}, u32[]{:S(2)}, u32[]{:S(2)}) async-start(bf16[1,32,2]{2,0,1:T(2,128)(2,1)} %all_to_all.12), calls=%async_computation | async-start | bytes 32768 | tf_op jit(solution)/shard_map/all_to_all | solution.py:74
  21.8 0.8 convert_bitcast_fusion
  22.6 2.8 copy.42
  25.4 10.8 %all-to-all-done = bf16[1,32,2]{2,0,1:T(2,128)(2,1)S(1)} async-done(((bf16[1,32,2]{2,0,1:T(2,128)(2,1)}), bf16[1,32,2]{2,0,1:T(2,128)(2,1)S(1)}, u32[]{:S(2)}, u32[]{:S(2)}) %all-to-all-start) | async-done | bytes 160 | tf_op jit(solution)/shard_map/all_to_all | solution.py:74
  36.3 4.8 all-to-all-start.1
  41.8 4.0 collective-permute-start.3
  45.8 1.9 collective-permute-start.2
  47.7 1.1 fusion.119
  48.8 1.3 collective-permute-start.1
  50.1 3.8 collective-permute-start
  54.1 0.7 fusion.125
  56.8 0.9 slice_bitcast_fusion.2
  57.7 67.6 %collective-permute-done.3 = f32[1,4,8,128]{3,2,1,0:T(8,128)S(1)} collective-permute-done((f32[1,4,8,128]{3,2,1,0:T(8,128)S(1)}, f32[1,4,8,128]{3,2,1,0:T(8,128)S(1)}, u32[]{:S(2)}, u32[]{:S(2)}) %collective-permute-start.3) | collective-permute-done | bytes 16416 | tf_op jit(solution)/shard_map/ppermute | solution.py:22
  125.4 1.3 collective-permute-start.5
  126.7 3.0 collective-permute-start.4
  130.6 1.5 fusion.39
  132.1 27.6 %collective-permute-start.9 = (f32[1,4,8,128]{3,2,1,0:T(8,128)S(1)}, f32[1,4,8,128]{3,2,1,0:T(8,128)S(1)}, u32[]{:S(2)}, u32[]{:S(2)}) collective-permute-start(f32[1,4,8,128]{3,2,1,0:T(8,128)S(1)} %bitcast.136), channel_id=1, source_target_pairs={{1,0},{2,1},{3,2},{4,3},{5,4},{6,5},{7,6},{8,7},{9,8},{10,9},{11,1... | collective-permute-start | bytes 49160 | tf_op jit(solution)/shard_map/ppermute | solution.py:22
  159.8 1.9 collective-permute-start.8
  161.9 6.2 collective-permute-done.8
  168.1 1.3 collective-permute-start.11
  169.4 10.4 %collective-permute-start.10 = (f32[1,12,4,128]{3,2,1,0:T(4,128)S(1)}, f32[1,12,4,128]{3,2,1,0:T(4,128)S(1)}, u32[]{:S(2)}, u32[]{:S(2)}) collective-permute-start(f32[1,12,4,128]{3,2,1,0:T(4,128)S(1)} %get-tuple-element.30), channel_id=1, source_target_pairs={{0,16},{16,32},{32,48},{48,64},{64,80},{80,96},{96,112},{112,128},... | collective-permute-start | bytes 73736 | tf_op jit(solution)/shard_map/ppermute | solution.py:19
  179.8 37.0 %all_gather.12 = f32[64,8,128]{2,1,0:T(8,128)} all-gather(f32[4,8,128]{2,1,0:T(8,128)S(1)} %get-tuple-element.14), channel_id=1, replica_groups=mesh['tile'=32,'dir'=16] {'dir'}, dimensions={0}, use_global_device_ids=true | all-gather | bytes 278528 | tf_op jit(solution)/shard_map/all_gather | solution.py:136
  216.8 1.5 fusion.108
  218.3 3.6 collective-permute-start.15
  221.9 2.2 collective-permute-start.14
  224.2 5.3 select_maximum_fusion.6
  229.5 3.0 fusion.6
  232.5 7.7 %multiply_add_fusion.3 = f32[4,64,8,128]{3,2,1,0:T(8,128)S(1)} fusion(f32[4,64,8,128]{3,2,1,0:T(8,128)S(1)} %bitcast.132, f32[4,72,16,136]{3,2,1,0:T(8,128)S(1)} %copy-done.2, f32[4,64,4,128]{3,2,1,0:T(4,128)S(1)} %copy-done.15, f32[4,64,8,128]{3,2,1,0:T(8,128)S(1)} %convert_element_type.62, f32[4,64,4,128]{3,2,1,0:T(4,128)} %collective-permute-done, ...), kind=kLoop, calls=%fused_computation.110 | loop fusion | flops 23855104 | bytes 22806528 | tf_op jit(solution)/shard_map/add | solution.py:143
  240.4 1.4 collective-permute-start.7
  241.9 3.1 collective-permute-start.6
  245.0 1.3 collective-permute-start.17
  246.3 7.5 collective-permute-start.16
  253.7 49.0 %all_gather.13 = f32[64,8,128]{2,1,0:T(8,128)S(1)} all-gather(f32[4,8,128]{2,1,0:T(8,128)S(1)} %get-tuple-element.12), channel_id=1, replica_groups=mesh['tile'=32,'dir'=16] {'dir'}, dimensions={0}, use_global_device_ids=true | all-gather | bytes 278528 | tf_op jit(solution)/shard_map/all_gather | solution.py:136
  302.8 2.7 select_maximum_fusion.4
  305.5 6.1 multiply_add_fusion.2
  311.8 1.3 collective-permute-start.13
  313.1 3.1 collective-permute-start.12
  316.1 2.2 fusion.42
  318.4 3.2 collective-permute-start.21
  321.5 3.0 collective-permute-start.20
  324.5 46.2 %all_gather.14 = f32[64,8,128]{2,1,0:T(8,128)S(1)} all-gather(f32[4,8,128]{2,1,0:T(8,128)S(1)} %get-tuple-element.10), channel_id=1, replica_groups=mesh['tile'=32,'dir'=16] {'dir'}, dimensions={0}, use_global_device_ids=true | all-gather | bytes 278528 | tf_op jit(solution)/shard_map/all_gather | solution.py:136
  370.7 1.3 collective-permute-start.23
  372.0 3.2 collective-permute-start.22
  375.2 2.7 select_maximum_fusion.2
  377.9 6.1 multiply_add_fusion.1
  384.0 1.0 copy-done.3
  384.9 1.1 fusion.116
  386.1 1.3 collective-permute-start.19
  387.4 11.4 %collective-permute-start.18 = (f32[4,64,4,128]{3,2,1,0:T(4,128)}, f32[4,64,4,128]{3,2,1,0:T(4,128)}, u32[]{:S(2)}, u32[]{:S(2)}) collective-permute-start(f32[4,64,4,128]{3,2,1,0:T(4,128)} %get-tuple-element.15), channel_id=1, source_target_pairs={{0,16},{16,32},{32,48},{48,64},{64,80},{80,96},{96,112},{112,128},... | collective-permute-start | bytes 1572872 | tf_op jit(solution)/shard_map/ppermute | solution.py:19
  398.9 0.9 fusion.56
  399.7 48.9 %all_gather.15 = f32[64,8,128]{2,1,0:T(8,128)} all-gather(f32[4,8,128]{2,1,0:T(8,128)S(1)} %fusion.56), channel_id=1, replica_groups=mesh['tile'=32,'dir'=16] {'dir'}, dimensions={0}, use_global_device_ids=true | all-gather | bytes 278528 | tf_op jit(solution)/shard_map/all_gather | solution.py:136
  448.6 15.9 %copy.45 = f32[4,64,8,128]{0,3,2,1:T(8,128)} copy(f32[4,64,8,128]{3,2,1,0:T(8,128)S(1)} %multiply_add_fusion.3) | data formatting | bytes 2097152 | tf_op jit(solution)/shard_map/add | solution.py:143
  464.6 11.3 %gather_fusion = f32[256,4]{1,0:T(8,128)S(1)} fusion(f32[4,65536]{0,1:T(8,128)} %bitcast.128, s32[1024]{0:T(1024)S(1)} %pad_clamp_fusion), kind=kCustom, calls=%fused_computation.clone | custom fusion | bytes 9216 | tf_op jit(solution)/shard_map/jit(_take)/gather | solution.py:149
  475.8 16.0 %copy.46 = f32[4,64,8,128]{0,3,2,1:T(8,128)} copy(f32[4,64,8,128]{3,2,1,0:T(8,128)S(1)} %multiply_add_fusion.2) | data formatting | bytes 2097152 | tf_op jit(solution)/shard_map/add | solution.py:143
  491.8 11.9 %gather_fusion.1 = f32[256,4]{1,0:T(8,128)} fusion(f32[4,65536]{0,1:T(8,128)} %bitcast.130, s32[1024]{0:T(1024)S(1)} %pad_clamp_fusion), kind=kCustom, calls=%fused_computation.1.clone | custom fusion | bytes 9216 | tf_op jit(solution)/shard_map/jit(_take)/gather | solution.py:149
  503.7 16.0 %copy.47 = f32[4,64,8,128]{0,3,2,1:T(8,128)} copy(f32[4,64,8,128]{3,2,1,0:T(8,128)S(1)} %copy-done.4) | data formatting | bytes 2097152 | tf_op jit(solution)/shard_map/add | solution.py:143
  519.7 11.9 %gather_fusion.2 = f32[256,4]{1,0:T(8,128)} fusion(f32[4,65536]{0,1:T(8,128)} %bitcast.131, s32[1024]{0:T(1024)S(1)} %pad_clamp_fusion), kind=kCustom, calls=%fused_computation.2.clone | custom fusion | bytes 9216 | tf_op jit(solution)/shard_map/jit(_take)/gather | solution.py:149
  531.6 3.8 select_maximum_fusion
  535.4 8.5 %multiply_add_fusion = f32[4,64,8,128]{3,2,1,0:T(8,128)} fusion(f32[4,64,8,128]{3,2,1,0:T(8,128)S(1)} %bitcast.135, f32[4,72,16,136]{3,2,1,0:T(8,128)S(1)} %select_maximum_fusion, f32[4,64,4,128]{3,2,1,0:T(4,128)} %collective-permute-done.19, f32[4,64,8,128]{3,2,1,0:T(8,128)S(1)} %copy-done.4, f32[4,64,4,128]{3,2,1,0:T(4,128)} %collective-permute-done.18, ...), kind=kLoop, calls=%fused_computation.107 | loop fusion | flops 23592960 | bytes 23330816 | tf_op jit(solution)/shard_map/add | solution.py:143
  543.9 16.9 %copy.48 = f32[4,64,8,128]{0,3,2,1:T(8,128)} copy(f32[4,64,8,128]{3,2,1,0:T(8,128)} %multiply_add_fusion) | data formatting | bytes 2097152 | tf_op jit(solution)/shard_map/add | solution.py:143
  560.8 11.3 %gather_fusion.3 = f32[256,4]{1,0:T(8,128)S(1)} fusion(f32[4,65536]{0,1:T(8,128)} %bitcast.129, s32[1024]{0:T(1024)S(1)} %pad_clamp_fusion), kind=kCustom, calls=%fused_computation.3.clone | custom fusion | bytes 9216 | tf_op jit(solution)/shard_map/jit(_take)/gather | solution.py:149
  572.6 173.6 %psum.7 = f32[4,4,256]{2,1,0:T(4,128)} all-reduce(f32[4,4,256]{2,1,0:T(4,128)S(1)} %pad_maximum_fusion.12), channel_id=1, replica_groups=mesh['tile'=32,'dir'=16] {'tile'}, use_global_device_ids=true, to_apply=%region_1.3 | all-reduce | flops 4096 | bytes 32768 | tf_op jit(solution)/shard_map/psum | solution.py:153
  (111 shorter events, 6.3 us)
Async XLA Ops:
  0.6 21.2 %copy-start = (bf16[4,32,32,128]{3,2,1,0:T(8,128)(2,1)S(1)}, bf16[4,32,32,128]{3,2,1,0:T(8,128)(2,1)}, u32[]{:S(2)}) copy-start(bf16[4,32,32,128]{3,2,1,0:T(8,128)(2,1)} %param.22) | copy-start | bytes 3145732
  3.8 32.4 %all-to-all-start = ((bf16[1,32,2]{2,0,1:T(2,128)(2,1)}), bf16[1,32,2]{2,0,1:T(2,128)(2,1)S(1)}, u32[]{:S(2)}, u32[]{:S(2)}) async-start(bf16[1,32,2]{2,0,1:T(2,128)(2,1)} %all_to_all.12), calls=%async_computation | async-start | bytes 32768 | tf_op jit(solution)/shard_map/all_to_all | solution.py:74
  22.6 25.1 %copy-start.5 = (bf16[4,64,8,128]{3,2,1,0:T(8,128)(2,1)S(1)}, bf16[4,64,8,128]{3,2,1,0:T(8,128)(2,1)}, u32[]{:S(2)}) copy-start(bf16[4,64,8,128]{3,2,1,0:T(8,128)(2,1)} %param.21) | copy-start | bytes 1572868
  22.6 31.3 %copy-start.17 = (bf16[3,64,8,128]{3,2,1,0:T(8,128)(2,1)S(1)}, bf16[3,64,8,128]{3,2,1,0:T(8,128)(2,1)}, u32[]{:S(2)}) copy-start(bf16[3,64,8,128]{3,2,1,0:T(8,128)(2,1)} %param.19) | copy-start | bytes 1179652
  25.4 28.6 %copy-start.21 = (s32[3]{0:T(128)S(1)}, s32[3]{0:T(128)}, u32[]{:S(2)}) copy-start(s32[3]{0:T(128)} %param.26) | copy-start | bytes 40
  25.4 30.6 %copy-start.22 = (f32[4]{0:T(128)S(1)}, f32[4]{0:T(128)}, u32[]{:S(2)}) copy-start(f32[4]{0:T(128)} %param.25) | copy-start | bytes 52
  25.4 31.4 %copy-start.23 = (s32[256]{0:T(256)S(1)}, s32[256]{0:T(256)}, u32[]{:S(2)}) copy-start(s32[256]{0:T(256)} %param.29) | copy-start | bytes 3076
  25.4 31.4 %copy-start.24 = (s32[256]{0:T(256)S(1)}, s32[256]{0:T(256)}, u32[]{:S(2)}) copy-start(s32[256]{0:T(256)} %param.28) | copy-start | bytes 3076
  25.4 31.4 %copy-start.25 = (s32[256]{0:T(256)S(1)}, s32[256]{0:T(256)}, u32[]{:S(2)}) copy-start(s32[256]{0:T(256)} %param.27) | copy-start | bytes 3076
  25.4 105.0 %copy-start.20 = (bf16[64,8,128]{2,1,0:T(8,128)(2,1)S(1)}, bf16[64,8,128]{2,1,0:T(8,128)(2,1)}, u32[]{:S(2)}) copy-start(bf16[64,8,128]{2,1,0:T(8,128)(2,1)} %param.18) | copy-start | bytes 393220
  36.3 193.2 %all-to-all-start.1 = ((bf16[4,64,32,128]{3,2,0,1:T(8,128)(2,1)}), bf16[4,64,32,128]{3,2,0,1:T(8,128)(2,1)}, u32[]{:S(2)}, u32[]{:S(2)}) async-start(bf16[4,64,32,128]{3,2,0,1:T(8,128)(2,1)} %copy.42), calls=%async_computation.1 | async-start | bytes 4194304 | tf_op jit(solution)/shard_map/all_to_all | solution.py:73
  41.8 83.6 %collective-permute-start.3 = (f32[1,4,8,128]{3,2,1,0:T(8,128)S(1)}, f32[1,4,8,128]{3,2,1,0:T(8,128)S(1)}, u32[]{:S(2)}, u32[]{:S(2)}) collective-permute-start(f32[1,4,8,128]{3,2,1,0:T(8,128)S(1)} %dynamic-slice_bitcast_fusion.3), channel_id=1, source_target_pairs={{1,0},{2,1},{3,2},{4,3},{5,4},{6,5},{7,6},{8,7},{9,8},{10,9},{11,1... | collective-permute-start | bytes 49160 | tf_op jit(solution)/shard_map/ppermute | solution.py:22
  45.8 79.6 %collective-permute-start.2 = (f32[1,4,8,128]{3,2,1,0:T(8,128)S(1)}, f32[1,4,8,128]{3,2,1,0:T(8,128)S(1)}, u32[]{:S(2)}, u32[]{:S(2)}) collective-permute-start(f32[1,4,8,128]{3,2,1,0:T(8,128)S(1)} %dynamic-slice_bitcast_fusion.3), channel_id=1, source_target_pairs={{0,1},{1,2},{2,3},{3,4},{4,5},{5,6},{6,7},{7,8},{8,9},{9,10},{10,1... | collective-permute-start | bytes 49160 | tf_op jit(solution)/shard_map/ppermute | solution.py:19
  48.8 175.3 %collective-permute-start.1 = (f32[4,64,4,128]{3,2,1,0:T(4,128)}, f32[4,64,4,128]{3,2,1,0:T(4,128)S(1)}, u32[]{:S(2)}, u32[]{:S(2)}) collective-permute-start(f32[4,64,4,128]{3,2,1,0:T(4,128)} %get-tuple-element.25), channel_id=1, source_target_pairs={{16,0},{32,16},{48,32},{64,48},{80,64},{96,80},{112,96},{128,112},... | collective-permute-start | bytes 1572872 | tf_op jit(solution)/shard_map/ppermute | solution.py:22
  50.1 174.0 %collective-permute-start = (f32[4,64,4,128]{3,2,1,0:T(4,128)}, f32[4,64,4,128]{3,2,1,0:T(4,128)}, u32[]{:S(2)}, u32[]{:S(2)}) collective-permute-start(f32[4,64,4,128]{3,2,1,0:T(4,128)} %get-tuple-element.24), channel_id=1, source_target_pairs={{0,16},{16,32},{32,48},{48,64},{64,80},{80,96},{96,112},{112,128},... | collective-permute-start | bytes 1572872 | tf_op jit(solution)/shard_map/ppermute | solution.py:19
  54.0 175.4 %copy-start.13 = (f32[3,64,8,128]{3,2,1,0:T(8,128)}, f32[3,64,8,128]{3,2,1,0:T(8,128)S(1)}, u32[]{:S(2)}) copy-start(f32[3,64,8,128]{3,2,1,0:T(8,128)S(1)} %convert_element_type.65) | copy-start | bytes 2359300
  125.4 5.1 collective-permute-start.5
  126.7 3.9 collective-permute-start.4
  132.1 29.7 %collective-permute-start.9 = (f32[1,4,8,128]{3,2,1,0:T(8,128)S(1)}, f32[1,4,8,128]{3,2,1,0:T(8,128)S(1)}, u32[]{:S(2)}, u32[]{:S(2)}) collective-permute-start(f32[1,4,8,128]{3,2,1,0:T(8,128)S(1)} %bitcast.136), channel_id=1, source_target_pairs={{1,0},{2,1},{3,2},{4,3},{5,4},{6,5},{7,6},{8,7},{9,8},{10,9},{11,1... | collective-permute-start | bytes 49160 | tf_op jit(solution)/shard_map/ppermute | solution.py:22
  159.8 8.3 %collective-permute-start.8 = (f32[1,4,8,128]{3,2,1,0:T(8,128)S(1)}, f32[1,4,8,128]{3,2,1,0:T(8,128)S(1)}, u32[]{:S(2)}, u32[]{:S(2)}) collective-permute-start(f32[1,4,8,128]{3,2,1,0:T(8,128)S(1)} %bitcast.137), channel_id=1, source_target_pairs={{0,1},{1,2},{2,3},{3,4},{4,5},{5,6},{6,7},{7,8},{8,9},{9,10},{10,1... | collective-permute-start | bytes 49160 | tf_op jit(solution)/shard_map/ppermute | solution.py:19
  168.1 48.6 %collective-permute-start.11 = (f32[1,12,4,128]{3,2,1,0:T(4,128)S(1)}, f32[1,12,4,128]{3,2,1,0:T(4,128)S(1)}, u32[]{:S(2)}, u32[]{:S(2)}) collective-permute-start(f32[1,12,4,128]{3,2,1,0:T(4,128)S(1)} %get-tuple-element.31), channel_id=1, source_target_pairs={{16,0},{32,16},{48,32},{64,48},{80,64},{96,80},{112,96},{128,112},... | collective-permute-start | bytes 73736 | tf_op jit(solution)/shard_map/ppermute | solution.py:22
  169.4 47.3 %collective-permute-start.10 = (f32[1,12,4,128]{3,2,1,0:T(4,128)S(1)}, f32[1,12,4,128]{3,2,1,0:T(4,128)S(1)}, u32[]{:S(2)}, u32[]{:S(2)}) collective-permute-start(f32[1,12,4,128]{3,2,1,0:T(4,128)S(1)} %get-tuple-element.30), channel_id=1, source_target_pairs={{0,16},{16,32},{32,48},{48,64},{64,80},{80,96},{96,112},{112,128},... | collective-permute-start | bytes 73736 | tf_op jit(solution)/shard_map/ppermute | solution.py:19
  218.3 26.6 %collective-permute-start.15 = (f32[1,4,8,128]{3,2,1,0:T(8,128)S(1)}, f32[1,4,8,128]{3,2,1,0:T(8,128)S(1)}, u32[]{:S(2)}, u32[]{:S(2)}) collective-permute-start(f32[1,4,8,128]{3,2,1,0:T(8,128)S(1)} %get-tuple-element.11), channel_id=1, source_target_pairs={{1,0},{2,1},{3,2},{4,3},{5,4},{6,5},{7,6},{8,7},{9,8},{10,9},{11,1... | collective-permute-start | bytes 49160 | tf_op jit(solution)/shard_map/ppermute | solution.py:22
  221.9 23.0 %collective-permute-start.14 = (f32[1,4,8,128]{3,2,1,0:T(8,128)S(1)}, f32[1,4,8,128]{3,2,1,0:T(8,128)S(1)}, u32[]{:S(2)}, u32[]{:S(2)}) collective-permute-start(f32[1,4,8,128]{3,2,1,0:T(8,128)S(1)} %get-tuple-element.11), channel_id=1, source_target_pairs={{0,1},{1,2},{2,3},{3,4},{4,5},{5,6},{6,7},{7,8},{8,9},{9,10},{10,1... | collective-permute-start | bytes 49160 | tf_op jit(solution)/shard_map/ppermute | solution.py:19
  224.2 5.3 copy-start.14
  229.5 3.1 copy-start.2
  229.5 3.1 copy-start.15
  240.2 65.2 %copy-start.6 = (bf16[4,64,8,128]{3,2,1,0:T(8,128)(2,1)S(1)}, bf16[4,64,8,128]{3,2,1,0:T(8,128)(2,1)}, u32[]{:S(2)}) copy-start(bf16[4,64,8,128]{3,2,1,0:T(8,128)(2,1)} %param.21) | copy-start | bytes 1572868
  240.2 65.2 %copy-start.7 = (f32[64,8,128]{2,1,0:T(8,128)S(1)}, f32[64,8,128]{2,1,0:T(8,128)}, u32[]{:S(2)}) copy-start(f32[64,8,128]{2,1,0:T(8,128)} %get-tuple-element.21) | copy-start | bytes 786436
  240.2 65.2 %copy-start.9 = (f32[64,8,128]{2,1,0:T(8,128)S(1)}, f32[64,8,128]{2,1,0:T(8,128)}, u32[]{:S(2)}) copy-start(f32[64,8,128]{2,1,0:T(8,128)} %get-tuple-element.22) | copy-start | bytes 786436
  240.2 65.2 %copy-start.11 = (f32[64,8,128]{2,1,0:T(8,128)S(1)}, f32[64,8,128]{2,1,0:T(8,128)}, u32[]{:S(2)}) copy-start(f32[64,8,128]{2,1,0:T(8,128)} %get-tuple-element.23) | copy-start | bytes 786436
  240.4 62.3 %collective-permute-start.7 = (f32[4,64,4,128]{3,2,1,0:T(4,128)S(1)}, f32[4,64,4,128]{3,2,1,0:T(4,128)S(1)}, u32[]{:S(2)}, u32[]{:S(2)}) collective-permute-start(f32[4,64,4,128]{3,2,1,0:T(4,128)S(1)} %get-tuple-element.20), channel_id=1, source_target_pairs={{16,0},{32,16},{48,32},{64,48},{80,64},{96,80},{112,96},{128,112},... | collective-permute-start | bytes 1572872 | tf_op jit(solution)/shard_map/ppermute | solution.py:22
  241.9 60.9 %collective-permute-start.6 = (f32[4,64,4,128]{3,2,1,0:T(4,128)S(1)}, f32[4,64,4,128]{3,2,1,0:T(4,128)S(1)}, u32[]{:S(2)}, u32[]{:S(2)}) collective-permute-start(f32[4,64,4,128]{3,2,1,0:T(4,128)S(1)} %get-tuple-element.19), channel_id=1, source_target_pairs={{0,16},{16,32},{32,48},{48,64},{64,80},{80,96},{96,112},{112,128},... | collective-permute-start | bytes 1572872 | tf_op jit(solution)/shard_map/ppermute | solution.py:19
  245.0 57.7 %collective-permute-start.17 = (f32[1,12,4,128]{3,2,1,0:T(4,128)S(1)}, f32[1,12,4,128]{3,2,1,0:T(4,128)S(1)}, u32[]{:S(2)}, u32[]{:S(2)}) collective-permute-start(f32[1,12,4,128]{3,2,1,0:T(4,128)S(1)} %get-tuple-element.29), channel_id=1, source_target_pairs={{16,0},{32,16},{48,32},{64,48},{80,64},{96,80},{112,96},{128,112},... | collective-permute-start | bytes 73736 | tf_op jit(solution)/shard_map/ppermute | solution.py:22
  246.3 56.4 %collective-permute-start.16 = (f32[1,12,4,128]{3,2,1,0:T(4,128)S(1)}, f32[1,12,4,128]{3,2,1,0:T(4,128)S(1)}, u32[]{:S(2)}, u32[]{:S(2)}) collective-permute-start(f32[1,12,4,128]{3,2,1,0:T(4,128)S(1)} %get-tuple-element.28), channel_id=1, source_target_pairs={{0,16},{16,32},{32,48},{48,64},{64,80},{80,96},{96,112},{112,128},... | collective-permute-start | bytes 73736 | tf_op jit(solution)/shard_map/ppermute | solution.py:19
  311.8 63.4 %collective-permute-start.13 = (f32[4,64,4,128]{3,2,1,0:T(4,128)S(1)}, f32[4,64,4,128]{3,2,1,0:T(4,128)S(1)}, u32[]{:S(2)}, u32[]{:S(2)}) collective-permute-start(f32[4,64,4,128]{3,2,1,0:T(4,128)S(1)} %get-tuple-element.18), channel_id=1, source_target_pairs={{16,0},{32,16},{48,32},{64,48},{80,64},{96,80},{112,96},{128,112},... | collective-permute-start | bytes 1572872 | tf_op jit(solution)/shard_map/ppermute | solution.py:22
  313.1 62.1 %collective-permute-start.12 = (f32[4,64,4,128]{3,2,1,0:T(4,128)S(1)}, f32[4,64,4,128]{3,2,1,0:T(4,128)S(1)}, u32[]{:S(2)}, u32[]{:S(2)}) collective-permute-start(f32[4,64,4,128]{3,2,1,0:T(4,128)S(1)} %get-tuple-element.17), channel_id=1, source_target_pairs={{0,16},{16,32},{32,48},{48,64},{64,80},{80,96},{96,112},{112,128},... | collective-permute-start | bytes 1572872 | tf_op jit(solution)/shard_map/ppermute | solution.py:19
  318.4 52.3 %collective-permute-start.21 = (f32[1,4,8,128]{3,2,1,0:T(8,128)S(1)}, f32[1,4,8,128]{3,2,1,0:T(8,128)S(1)}, u32[]{:S(2)}, u32[]{:S(2)}) collective-permute-start(f32[1,4,8,128]{3,2,1,0:T(8,128)S(1)} %get-tuple-element.9), channel_id=1, source_target_pairs={{1,0},{2,1},{3,2},{4,3},{5,4},{6,5},{7,6},{8,7},{9,8},{10,9},{11,1... | collective-permute-start | bytes 49160 | tf_op jit(solution)/shard_map/ppermute | solution.py:22
  321.5 49.1 %collective-permute-start.20 = (f32[1,4,8,128]{3,2,1,0:T(8,128)S(1)}, f32[1,4,8,128]{3,2,1,0:T(8,128)S(1)}, u32[]{:S(2)}, u32[]{:S(2)}) collective-permute-start(f32[1,4,8,128]{3,2,1,0:T(8,128)S(1)} %get-tuple-element.9), channel_id=1, source_target_pairs={{0,1},{1,2},{2,3},{3,4},{4,5},{5,6},{6,7},{7,8},{8,9},{9,10},{10,1... | collective-permute-start | bytes 49160 | tf_op jit(solution)/shard_map/ppermute | solution.py:19
  370.7 28.1 %collective-permute-start.23 = (f32[1,12,4,128]{3,2,1,0:T(4,128)S(1)}, f32[1,12,4,128]{3,2,1,0:T(4,128)S(1)}, u32[]{:S(2)}, u32[]{:S(2)}) collective-permute-start(f32[1,12,4,128]{3,2,1,0:T(4,128)S(1)} %get-tuple-element.27), channel_id=1, source_target_pairs={{16,0},{32,16},{48,32},{64,48},{80,64},{96,80},{112,96},{128,112},... | collective-permute-start | bytes 73736 | tf_op jit(solution)/shard_map/ppermute | solution.py:22
  372.0 26.8 %collective-permute-start.22 = (f32[1,12,4,128]{3,2,1,0:T(4,128)S(1)}, f32[1,12,4,128]{3,2,1,0:T(4,128)S(1)}, u32[]{:S(2)}, u32[]{:S(2)}) collective-permute-start(f32[1,12,4,128]{3,2,1,0:T(4,128)S(1)} %get-tuple-element.26), channel_id=1, source_target_pairs={{0,16},{16,32},{32,48},{48,64},{64,80},{80,96},{96,112},{112,128},... | collective-permute-start | bytes 73736 | tf_op jit(solution)/shard_map/ppermute | solution.py:19
  384.0 1.0 copy-start.3
  386.1 145.5 %collective-permute-start.19 = (f32[4,64,4,128]{3,2,1,0:T(4,128)}, f32[4,64,4,128]{3,2,1,0:T(4,128)}, u32[]{:S(2)}, u32[]{:S(2)}) collective-permute-start(f32[4,64,4,128]{3,2,1,0:T(4,128)} %get-tuple-element.16), channel_id=1, source_target_pairs={{16,0},{32,16},{48,32},{64,48},{80,64},{96,80},{112,96},{128,112},... | collective-permute-start | bytes 1572872 | tf_op jit(solution)/shard_map/ppermute | solution.py:22
  387.4 144.2 %collective-permute-start.18 = (f32[4,64,4,128]{3,2,1,0:T(4,128)}, f32[4,64,4,128]{3,2,1,0:T(4,128)}, u32[]{:S(2)}, u32[]{:S(2)}) collective-permute-start(f32[4,64,4,128]{3,2,1,0:T(4,128)} %get-tuple-element.15), channel_id=1, source_target_pairs={{0,16},{16,32},{32,48},{48,64},{64,80},{80,96},{96,112},{112,128},... | collective-permute-start | bytes 1572872 | tf_op jit(solution)/shard_map/ppermute | solution.py:19
  475.8 27.9 %copy-start.4 = (f32[4,64,8,128]{3,2,1,0:T(8,128)S(1)}, f32[4,64,8,128]{3,2,1,0:T(8,128)}, u32[]{:S(2)}) copy-start(f32[4,64,8,128]{3,2,1,0:T(8,128)} %copy-done.3) | copy-start | bytes 3145732
  531.5 3.8 copy-start.8
  531.5 3.8 copy-start.10
  531.5 3.8 copy-start.12
  531.5 3.8 copy-start.16
  543.9 28.2 %copy-start.18 = (f32[256,4]{1,0:T(8,128)S(1)}, f32[256,4]{1,0:T(8,128)}, u32[]{:S(2)}) copy-start(f32[256,4]{1,0:T(8,128)} %gather_fusion.1) | copy-start | bytes 12292
  543.9 28.2 %copy-start.19 = (f32[256,4]{1,0:T(8,128)S(1)}, f32[256,4]{1,0:T(8,128)}, u32[]{:S(2)}) copy-start(f32[256,4]{1,0:T(8,128)} %gather_fusion.2) | copy-start | bytes 12292
  543.9 202.3 %copy-start.1 = (bf16[4,32,32,128]{3,2,1,0:T(8,128)(2,1)S(1)}, bf16[4,32,32,128]{3,2,1,0:T(8,128)(2,1)}, u32[]{:S(2)}) copy-start(bf16[4,32,32,128]{3,2,1,0:T(8,128)(2,1)} %param.22) | copy-start | bytes 3145732
where the time goes:
time: 748 us; the launch traced here: 746 us
  blocking collectives  355 us (47%)
  starting transfers between devices  126 us (17%)
  local copies, waits for them, and re-layouts  122 us (16%)
  waiting for transfers between devices  84.8 us (11%)
  other arithmetic  52.8 us (7%)
    all_gather x4, blocking collectives, local(): acceleration = lax.all_gather(local_accel, 'dir', axis=0, tiled=True)  181 us
    psum x1, blocking collectives, local(): traces = lax.psum(jnp.stack(records, axis=1), 'tile')  174 us
    ppermute x12, waiting for transfers between devices, padded_2(): lax.ppermute(lax.slice_in_dim(block, 0, width, axis=dim), axis, backward)  67.6 us
    add x4, local copies, waits for them, and re-layouts, local(): 2.0 * current_born - earlier_born  64.7 us
    ppermute x12, starting transfers between devices, padded_2(): lax.ppermute(lax.slice_in_dim(block, block.shape[dim] - width, None, axis...  54.4 us
    ppermute x12, starting transfers between devices, padded_2(): lax.ppermute(lax.slice_in_dim(block, 0, width, axis=dim), axis, backward)  48.9 us
    gather x4, local copies, waits for them, and re-layouts, local(): jnp.take(following.reshape(following.shape[0], -1), flat_index, axis=1)  46.3 us
    add x4, other arithmetic, local(): 2.0 * current_born - earlier_born  28.4 us
  transfers between devices with their start and end apart: 26, of which 4 were waited for; matrix products, arithmetic and copies ran while one was open for 17% of the time, Pallas kernels for 0%

commit v1 on v0

--- a/solution.py
+++ b/solution.py
@@ -133,7 +133,9 @@
         local_accel = operate(
             jnp.pad(back_wide[0], ((0, 0), (0, 0), (4, 4))), slab_stiff, slab_drift
         )
-        acceleration = lax.all_gather(local_accel, "dir", axis=0, tiled=True)
+        acceleration = jnp.concatenate(
+            lax.all_to_all(jnp.stack([local_accel] * lax.axis_size("dir")), "dir", 0, 0), axis=0
+        )
         previous, present = (
             present,
             2.0 * present - previous + local_accel + wavelet[step_index] * source_mask,

time: 748 us -> 723 us (0.967)
  blocking collectives: 355 us -> 172 us
  other arithmetic: 52.8 us -> 143 us
  starting transfers between devices: 126 us -> 181 us
  waiting for transfers between devices: 84.8 us -> 92.9 us
    all_gather x4 -> x0, blocking collectives: 181 us -> none  [local(): acceleration = lax.all_gather(local_accel, 'dir', axis=0, tiled=True)]
    add x4, other arithmetic: 28.4 us -> 114 us  [local(): 2.0 * current_born - earlier_born]
    all_to_all x0 -> x4, starting transfers between devices: none -> 30.6 us  [local(): lax.all_to_all(jnp.stack([local_accel] * lax.axis_size('dir')), 'dir', 0, 0)]
    ppermute x12, starting transfers between devices: 54.4 us -> 70.3 us  [padded_2(): lax.ppermute(lax.slice_in_dim(block, block.shape[dim] - width, None, axis...]
    ppermute x12, starting transfers between devices: 48.9 us -> 57.5 us  [padded_2(): lax.ppermute(lax.slice_in_dim(block, 0, width, axis=dim), axis, backward)]
  transfers between devices with their start and end apart: 26 -> 30, of which waited for: 4 -> 8; matrix products, arithmetic and copies ran while one was open for 17% -> 17% of each run, Pallas kernels for 0% -> 0%
where the time goes in v1:
time: 723 us; the launch traced here: 721 us
  starting transfers between devices  181 us (25%)
  blocking collectives  172 us (24%)
  other arithmetic  143 us (20%)
  local copies, waits for them, and re-layouts  126 us (17%)
  waiting for transfers between devices  92.9 us (13%)
    psum x1, blocking collectives, local(): traces = lax.psum(jnp.stack(records, axis=1), 'tile')  172 us
    add x4, other arithmetic, local(): 2.0 * current_born - earlier_born  114 us
    ppermute x12, starting transfers between devices, padded_2(): lax.ppermute(lax.slice_in_dim(block, block.shape[dim] - width, None, axis...  70.3 us
    ppermute x12, waiting for transfers between devices, padded_2(): lax.ppermute(lax.slice_in_dim(block, 0, width, axis=dim), axis, backward)  68.5 us
    add x4, local copies, waits for them, and re-layouts, local(): 2.0 * current_born - earlier_born  64.7 us
    ppermute x12, starting transfers between devices, padded_2(): lax.ppermute(lax.slice_in_dim(block, 0, width, axis=dim), axis, backward)  57.5 us
    gather x4, local copies, waits for them, and re-layouts, local(): jnp.take(following.reshape(following.shape[0], -1), flat_index, axis=1)  46.3 us
    all_to_all x4, starting transfers between devices, local(): lax.all_to_all(jnp.stack([local_accel] * lax.axis_size('dir')), 'dir', 0, 0)  30.6 us
  transfers between devices with their start and end apart: 30, of which 8 were waited for; matrix products, arithmetic and copies ran while one was open for 17% of the time, Pallas kernels for 0%

profile of v1, /device:TPU:24, one launch (start us, length us, event | category | flops | bytes accessed | tf_op | source)
XLA Modules:
  0.0 720.9 jit_solution(7517748783054560155)
XLA Ops:
  0.6 0.9 convert_reduce_fusion.1
  3.8 17.9 %all-to-all-start = ((bf16[1,32,2]{2,0,1:T(2,128)(2,1)}), bf16[1,32,2]{2,0,1:T(2,128)(2,1)S(1)}, u32[]{:S(2)}, u32[]{:S(2)}) async-start(bf16[1,32,2]{2,0,1:T(2,128)(2,1)} %all_to_all.28), calls=%async_computation | async-start | bytes 32768 | tf_op jit(solution)/shard_map/all_to_all | solution.py:74
  22.6 2.7 copy.42
  25.3 10.9 %all-to-all-done = bf16[1,32,2]{2,0,1:T(2,128)(2,1)S(1)} async-done(((bf16[1,32,2]{2,0,1:T(2,128)(2,1)}), bf16[1,32,2]{2,0,1:T(2,128)(2,1)S(1)}, u32[]{:S(2)}, u32[]{:S(2)}) %all-to-all-start) | async-done | bytes 160 | tf_op jit(solution)/shard_map/all_to_all | solution.py:74
  36.3 4.8 all-to-all-start.1
  41.8 4.0 collective-permute-start.3
  45.8 1.9 collective-permute-start.2
  47.7 1.1 fusion.119
  48.9 1.3 collective-permute-start.1
  50.2 3.1 collective-permute-start
  55.4 0.9 slice_bitcast_fusion.2
  56.9 68.5 %collective-permute-done.3 = f32[1,4,8,128]{3,2,1,0:T(8,128)S(1)} collective-permute-done((f32[1,4,8,128]{3,2,1,0:T(8,128)S(1)}, f32[1,4,8,128]{3,2,1,0:T(8,128)S(1)}, u32[]{:S(2)}, u32[]{:S(2)}) %collective-permute-start.3) | collective-permute-done | bytes 16416 | tf_op jit(solution)/shard_map/ppermute | solution.py:22
  125.4 1.3 collective-permute-start.5
  126.7 3.0 collective-permute-start.4
  130.6 1.5 fusion.39
  132.1 27.6 %collective-permute-start.9 = (f32[1,4,8,128]{3,2,1,0:T(8,128)S(1)}, f32[1,4,8,128]{3,2,1,0:T(8,128)S(1)}, u32[]{:S(2)}, u32[]{:S(2)}) collective-permute-start(f32[1,4,8,128]{3,2,1,0:T(8,128)S(1)} %bitcast.140), channel_id=1, source_target_pairs={{1,0},{2,1},{3,2},{4,3},{5,4},{6,5},{7,6},{8,7},{9,8},{10,9},{11,1... | collective-permute-start | bytes 49160 | tf_op jit(solution)/shard_map/ppermute | solution.py:22
  159.8 1.9 collective-permute-start.8
  161.8 6.3 collective-permute-done.8
  168.1 1.3 collective-permute-start.11
  169.4 10.4 %collective-permute-start.10 = (f32[1,12,4,128]{3,2,1,0:T(4,128)S(1)}, f32[1,12,4,128]{3,2,1,0:T(4,128)S(1)}, u32[]{:S(2)}, u32[]{:S(2)}) collective-permute-start(f32[1,12,4,128]{3,2,1,0:T(4,128)S(1)} %get-tuple-element.30), channel_id=1, source_target_pairs={{0,16},{16,32},{32,48},{48,64},{64,80},{80,96},{96,112},{112,128},... | collective-permute-start | bytes 73736 | tf_op jit(solution)/shard_map/ppermute | solution.py:19
  181.3 4.5 all-to-all-start.2
  185.9 4.1 select_maximum_fusion.6
  190.0 2.8 fusion.6
  193.0 28.5 %multiply_add_fusion.3 = f32[4,64,8,128]{3,2,1,0:T(8,128)S(1)} fusion(f32[4,64,8,128]{3,2,1,0:T(8,128)S(1)} %bitcast.136, f32[4,72,16,136]{3,2,1,0:T(8,128)} %select_maximum_fusion.6, f32[4,64,4,128]{3,2,1,0:T(4,128)} %copy-done.6, f32[4,64,8,128]{3,2,1,0:T(8,128)S(1)} %convert_element_type.62, f32[4,64,4,128]{3,2,1,0:T(4,128)} %copy-done.7, ...), kind=kLoop, calls=%fused_computation.110 | loop fusion | flops 23855104 | bytes 22806528 | tf_op jit(solution)/shard_map/add | solution.py:145
  221.5 1.1 fusion.118
  222.6 1.3 collective-permute-start.7
  223.9 7.9 %collective-permute-start.6 = (f32[4,64,4,128]{3,2,1,0:T(4,128)}, f32[4,64,4,128]{3,2,1,0:T(4,128)S(1)}, u32[]{:S(2)}, u32[]{:S(2)}) collective-permute-start(f32[4,64,4,128]{3,2,1,0:T(4,128)} %get-tuple-element.19), channel_id=1, source_target_pairs={{0,16},{16,32},{32,48},{48,64},{64,80},{80,96},{96,112},{112,128},... | collective-permute-start | bytes 1572872 | tf_op jit(solution)/shard_map/ppermute | solution.py:19
  231.8 1.5 fusion.108
  233.3 5.3 collective-permute-start.15
  238.6 1.9 collective-permute-start.14
  241.3 8.7 %all-to-all-start.3 = ((f32[16,4,8,128]{3,2,1,0:T(8,128)}), f32[16,4,8,128]{3,2,1,0:T(8,128)}, u32[]{:S(2)}, u32[]{:S(2)}) async-start(f32[16,4,8,128]{3,2,1,0:T(8,128)} %stack.19), calls=%async_computation.3 | async-start | bytes 524288 | tf_op jit(solution)/shard_map/all_to_all | solution.py:137
  250.1 1.3 collective-permute-start.17
  251.4 8.3 %collective-permute-start.16 = (f32[1,12,4,128]{3,2,1,0:T(4,128)S(1)}, f32[1,12,4,128]{3,2,1,0:T(4,128)S(1)}, u32[]{:S(2)}, u32[]{:S(2)}) collective-permute-start(f32[1,12,4,128]{3,2,1,0:T(4,128)S(1)} %get-tuple-element.28), channel_id=1, source_target_pairs={{0,16},{16,32},{32,48},{48,64},{64,80},{80,96},{96,112},{112,128},... | collective-permute-start | bytes 73736 | tf_op jit(solution)/shard_map/ppermute | solution.py:19
  261.2 4.1 select_maximum_fusion.4
  265.3 4.8 all-to-all-done.3
  270.1 28.1 %multiply_add_fusion.2 = f32[4,64,8,128]{3,2,1,0:T(8,128)S(1)} fusion(f32[4,64,8,128]{3,2,1,0:T(8,128)S(1)} %bitcast.137, f32[4,72,16,136]{3,2,1,0:T(8,128)} %select_maximum_fusion.4, f32[4,64,4,128]{3,2,1,0:T(4,128)} %copy-done.8, f32[4,64,8,128]{3,2,1,0:T(8,128)S(1)} %multiply_add_fusion.3, f32[4,64,4,128]{3,2,1,0:T(4,128)} %copy-done.9, ...), kind=kLoop, calls=%fused_computation.109 | loop fusion | flops 23855104 | bytes 22806528 | tf_op jit(solution)/shard_map/add | solution.py:145
  298.2 1.1 fusion.117
  299.4 1.3 collective-permute-start.13
  300.7 9.4 %collective-permute-start.12 = (f32[4,64,4,128]{3,2,1,0:T(4,128)}, f32[4,64,4,128]{3,2,1,0:T(4,128)}, u32[]{:S(2)}, u32[]{:S(2)}) collective-permute-start(f32[4,64,4,128]{3,2,1,0:T(4,128)} %get-tuple-element.17), channel_id=1, source_target_pairs={{0,16},{16,32},{32,48},{48,64},{64,80},{80,96},{96,112},{112,128},... | collective-permute-start | bytes 1572872 | tf_op jit(solution)/shard_map/ppermute | solution.py:19
  310.1 2.1 fusion.42
  312.2 10.2 %collective-permute-start.21 = (f32[1,4,8,128]{3,2,1,0:T(8,128)S(1)}, f32[1,4,8,128]{3,2,1,0:T(8,128)S(1)}, u32[]{:S(2)}, u32[]{:S(2)}) collective-permute-start(f32[1,4,8,128]{3,2,1,0:T(8,128)S(1)} %get-tuple-element.9), channel_id=1, source_target_pairs={{1,0},{2,1},{3,2},{4,3},{5,4},{6,5},{7,6},{8,7},{9,8},{10,9},{11,1... | collective-permute-start | bytes 49160 | tf_op jit(solution)/shard_map/ppermute | solution.py:22
  322.4 1.9 collective-permute-start.20
  325.1 8.7 %all-to-all-start.4 = ((f32[16,4,8,128]{3,2,1,0:T(8,128)}), f32[16,4,8,128]{3,2,1,0:T(8,128)}, u32[]{:S(2)}, u32[]{:S(2)}) async-start(f32[16,4,8,128]{3,2,1,0:T(8,128)} %stack.20), calls=%async_computation.4 | async-start | bytes 524288 | tf_op jit(solution)/shard_map/all_to_all | solution.py:137
  333.8 1.3 collective-permute-start.23
  335.1 11.4 %collective-permute-start.22 = (f32[1,12,4,128]{3,2,1,0:T(4,128)S(1)}, f32[1,12,4,128]{3,2,1,0:T(4,128)S(1)}, u32[]{:S(2)}, u32[]{:S(2)}) collective-permute-start(f32[1,12,4,128]{3,2,1,0:T(4,128)S(1)} %get-tuple-element.26), channel_id=1, source_target_pairs={{0,16},{16,32},{32,48},{48,64},{64,80},{80,96},{96,112},{112,128},... | collective-permute-start | bytes 73736 | tf_op jit(solution)/shard_map/ppermute | solution.py:19
  347.4 5.1 select_maximum_fusion.2
  352.6 28.0 %multiply_add_fusion.1 = f32[4,64,8,128]{3,2,1,0:T(8,128)S(1)} fusion(f32[4,64,8,128]{3,2,1,0:T(8,128)S(1)} %bitcast.138, f32[4,72,16,136]{3,2,1,0:T(8,128)} %select_maximum_fusion.2, f32[4,64,4,128]{3,2,1,0:T(4,128)} %collective-permute-done.13, f32[4,64,8,128]{3,2,1,0:T(8,128)S(1)} %multiply_add_fusion.2, f32[4,64,4,128]{3,2,1,0:T(4,128)} %collective-permute-done.12, ...), kind=kLoop, calls=%fused_computation.108 | loop fusion | flops 23592960 | bytes 23330816 | tf_op jit(solution)/shard_map/add | solution.py:145
  380.6 1.0 copy-done.2
  381.6 1.2 fusion.116
  382.7 1.3 collective-permute-start.19
  384.0 9.1 %collective-permute-start.18 = (f32[4,64,4,128]{3,2,1,0:T(4,128)}, f32[4,64,4,128]{3,2,1,0:T(4,128)}, u32[]{:S(2)}, u32[]{:S(2)}) collective-permute-start(f32[4,64,4,128]{3,2,1,0:T(4,128)} %get-tuple-element.15), channel_id=1, source_target_pairs={{0,16},{16,32},{32,48},{48,64},{64,80},{80,96},{96,112},{112,128},... | collective-permute-start | bytes 1572872 | tf_op jit(solution)/shard_map/ppermute | solution.py:19
  393.1 0.9 fusion.56
  394.7 8.7 %all-to-all-start.5 = ((f32[16,4,8,128]{3,2,1,0:T(8,128)}), f32[16,4,8,128]{3,2,1,0:T(8,128)}, u32[]{:S(2)}, u32[]{:S(2)}) async-start(f32[16,4,8,128]{3,2,1,0:T(8,128)} %stack.21), calls=%async_computation.5 | async-start | bytes 524288 | tf_op jit(solution)/shard_map/all_to_all | solution.py:137
  403.4 16.0 %copy.45 = f32[4,64,8,128]{0,3,2,1:T(8,128)} copy(f32[4,64,8,128]{3,2,1,0:T(8,128)S(1)} %multiply_add_fusion.3) | data formatting | bytes 2097152 | tf_op jit(solution)/shard_map/add | solution.py:145
  419.4 11.3 %gather_fusion = f32[256,4]{1,0:T(8,128)S(1)} fusion(f32[4,65536]{0,1:T(8,128)} %bitcast.132, s32[1024]{0:T(1024)S(1)} %pad_clamp_fusion), kind=kCustom, calls=%fused_computation.clone | custom fusion | bytes 9216 | tf_op jit(solution)/shard_map/jit(_take)/gather | solution.py:151
  430.7 16.0 %copy.46 = f32[4,64,8,128]{0,3,2,1:T(8,128)} copy(f32[4,64,8,128]{3,2,1,0:T(8,128)S(1)} %multiply_add_fusion.2) | data formatting | bytes 2097152 | tf_op jit(solution)/shard_map/add | solution.py:145
  446.6 11.9 %gather_fusion.1 = f32[256,4]{1,0:T(8,128)} fusion(f32[4,65536]{0,1:T(8,128)} %bitcast.134, s32[1024]{0:T(1024)S(1)} %pad_clamp_fusion), kind=kCustom, calls=%fused_computation.1.clone | custom fusion | bytes 9216 | tf_op jit(solution)/shard_map/jit(_take)/gather | solution.py:151
  458.5 15.9 %copy.47 = f32[4,64,8,128]{0,3,2,1:T(8,128)} copy(f32[4,64,8,128]{3,2,1,0:T(8,128)S(1)} %copy-done.3) | data formatting | bytes 2097152 | tf_op jit(solution)/shard_map/add | solution.py:145
  474.5 11.9 %gather_fusion.2 = f32[256,4]{1,0:T(8,128)} fusion(f32[4,65536]{0,1:T(8,128)} %bitcast.135, s32[1024]{0:T(1024)S(1)} %pad_clamp_fusion), kind=kCustom, calls=%fused_computation.2.clone | custom fusion | bytes 9216 | tf_op jit(solution)/shard_map/jit(_take)/gather | solution.py:151
  486.4 5.1 select_maximum_fusion
  491.5 29.0 %multiply_add_fusion = f32[4,64,8,128]{3,2,1,0:T(8,128)} fusion(f32[4,64,8,128]{3,2,1,0:T(8,128)S(1)} %bitcast.139, f32[4,72,16,136]{3,2,1,0:T(8,128)} %select_maximum_fusion, f32[4,64,4,128]{3,2,1,0:T(4,128)} %collective-permute-done.19, f32[4,64,8,128]{3,2,1,0:T(8,128)S(1)} %copy-done.3, f32[4,64,4,128]{3,2,1,0:T(4,128)} %collective-permute-done.18, ...), kind=kLoop, calls=%fused_computation.107 | loop fusion | flops 23592960 | bytes 23330816 | tf_op jit(solution)/shard_map/add | solution.py:145
  520.5 16.9 %copy.48 = f32[4,64,8,128]{0,3,2,1:T(8,128)} copy(f32[4,64,8,128]{3,2,1,0:T(8,128)} %multiply_add_fusion) | data formatting | bytes 2097152 | tf_op jit(solution)/shard_map/add | solution.py:145
  537.4 11.3 %gather_fusion.3 = f32[256,4]{1,0:T(8,128)S(1)} fusion(f32[4,65536]{0,1:T(8,128)} %bitcast.133, s32[1024]{0:T(1024)S(1)} %pad_clamp_fusion), kind=kCustom, calls=%fused_computation.3.clone | custom fusion | bytes 9216 | tf_op jit(solution)/shard_map/jit(_take)/gather | solution.py:151
  549.2 171.8 %psum.7 = f32[4,4,256]{2,1,0:T(4,128)} all-reduce(f32[4,4,256]{2,1,0:T(4,128)S(1)} %pad_maximum_fusion.12), channel_id=1, replica_groups=mesh['tile'=32,'dir'=16] {'tile'}, use_global_device_ids=true, to_apply=%region_1.3 | all-reduce | flops 4096 | bytes 32768 | tf_op jit(solution)/shard_map/psum | solution.py:155
  (121 shorter events, 14.2 us)
Async XLA Ops:
  0.6 21.2 %copy-start = (bf16[4,32,32,128]{3,2,1,0:T(8,128)(2,1)S(1)}, bf16[4,32,32,128]{3,2,1,0:T(8,128)(2,1)}, u32[]{:S(2)}) copy-start(bf16[4,32,32,128]{3,2,1,0:T(8,128)(2,1)} %param.22) | copy-start | bytes 3145732
  3.8 32.4 %all-to-all-start = ((bf16[1,32,2]{2,0,1:T(2,128)(2,1)}), bf16[1,32,2]{2,0,1:T(2,128)(2,1)S(1)}, u32[]{:S(2)}, u32[]{:S(2)}) async-start(bf16[1,32,2]{2,0,1:T(2,128)(2,1)} %all_to_all.28), calls=%async_computation | async-start | bytes 32768 | tf_op jit(solution)/shard_map/all_to_all | solution.py:74
  22.6 25.1 %copy-start.4 = (bf16[4,64,8,128]{3,2,1,0:T(8,128)(2,1)S(1)}, bf16[4,64,8,128]{3,2,1,0:T(8,128)(2,1)}, u32[]{:S(2)}) copy-start(bf16[4,64,8,128]{3,2,1,0:T(8,128)(2,1)} %param.21) | copy-start | bytes 1572868
  22.6 30.6 %copy-start.10 = (bf16[3,64,8,128]{3,2,1,0:T(8,128)(2,1)S(1)}, bf16[3,64,8,128]{3,2,1,0:T(8,128)(2,1)}, u32[]{:S(2)}) copy-start(bf16[3,64,8,128]{3,2,1,0:T(8,128)(2,1)} %param.19) | copy-start | bytes 1179652
  25.3 28.0 %copy-start.16 = (s32[3]{0:T(128)S(1)}, s32[3]{0:T(128)}, u32[]{:S(2)}) copy-start(s32[3]{0:T(128)} %param.26) | copy-start | bytes 40
  25.3 30.9 %copy-start.17 = (f32[4]{0:T(128)S(1)}, f32[4]{0:T(128)}, u32[]{:S(2)}) copy-start(f32[4]{0:T(128)} %param.25) | copy-start | bytes 52
  25.3 105.0 %copy-start.13 = (bf16[64,8,128]{2,1,0:T(8,128)(2,1)S(1)}, bf16[64,8,128]{2,1,0:T(8,128)(2,1)}, u32[]{:S(2)}) copy-start(bf16[64,8,128]{2,1,0:T(8,128)(2,1)} %param.18) | copy-start | bytes 393220
  36.3 144.4 %all-to-all-start.1 = ((bf16[4,64,32,128]{3,2,0,1:T(8,128)(2,1)}), bf16[4,64,32,128]{3,2,0,1:T(8,128)(2,1)}, u32[]{:S(2)}, u32[]{:S(2)}) async-start(bf16[4,64,32,128]{3,2,0,1:T(8,128)(2,1)} %copy.42), calls=%async_computation.1 | async-start | bytes 4194304 | tf_op jit(solution)/shard_map/all_to_all | solution.py:73
  41.8 83.6 %collective-permute-start.3 = (f32[1,4,8,128]{3,2,1,0:T(8,128)S(1)}, f32[1,4,8,128]{3,2,1,0:T(8,128)S(1)}, u32[]{:S(2)}, u32[]{:S(2)}) collective-permute-start(f32[1,4,8,128]{3,2,1,0:T(8,128)S(1)} %dynamic-slice_bitcast_fusion.3), channel_id=1, source_target_pairs={{1,0},{2,1},{3,2},{4,3},{5,4},{6,5},{7,6},{8,7},{9,8},{10,9},{11,1... | collective-permute-start | bytes 49160 | tf_op jit(solution)/shard_map/ppermute | solution.py:22
  45.8 79.6 %collective-permute-start.2 = (f32[1,4,8,128]{3,2,1,0:T(8,128)S(1)}, f32[1,4,8,128]{3,2,1,0:T(8,128)S(1)}, u32[]{:S(2)}, u32[]{:S(2)}) collective-permute-start(f32[1,4,8,128]{3,2,1,0:T(8,128)S(1)} %dynamic-slice_bitcast_fusion.3), channel_id=1, source_target_pairs={{0,1},{1,2},{2,3},{3,4},{4,5},{5,6},{6,7},{7,8},{8,9},{9,10},{10,1... | collective-permute-start | bytes 49160 | tf_op jit(solution)/shard_map/ppermute | solution.py:19
  48.9 137.0 %collective-permute-start.1 = (f32[4,64,4,128]{3,2,1,0:T(4,128)}, f32[4,64,4,128]{3,2,1,0:T(4,128)S(1)}, u32[]{:S(2)}, u32[]{:S(2)}) collective-permute-start(f32[4,64,4,128]{3,2,1,0:T(4,128)} %get-tuple-element.25), channel_id=1, source_target_pairs={{16,0},{32,16},{48,32},{64,48},{80,64},{96,80},{112,96},{128,112},... | collective-permute-start | bytes 1572872 | tf_op jit(solution)/shard_map/ppermute | solution.py:22
  50.2 135.7 %collective-permute-start = (f32[4,64,4,128]{3,2,1,0:T(4,128)}, f32[4,64,4,128]{3,2,1,0:T(4,128)S(1)}, u32[]{:S(2)}, u32[]{:S(2)}) collective-permute-start(f32[4,64,4,128]{3,2,1,0:T(4,128)} %get-tuple-element.24), channel_id=1, source_target_pairs={{0,16},{16,32},{32,48},{48,64},{64,80},{80,96},{96,112},{112,128},... | collective-permute-start | bytes 1572872 | tf_op jit(solution)/shard_map/ppermute | solution.py:19
  53.3 108.4 %copy-start.5 = (f32[3,64,8,128]{3,2,1,0:T(8,128)}, f32[3,64,8,128]{3,2,1,0:T(8,128)S(1)}, u32[]{:S(2)}) copy-start(f32[3,64,8,128]{3,2,1,0:T(8,128)S(1)} %convert_element_type.65) | copy-start | bytes 2359300
  55.4 106.4 %copy-start.18 = (pred[4,8]{1,0:T(4,128)(4,1)}, pred[4,8]{1,0:T(4,128)(4,1)S(1)}, u32[]{:S(2)}) copy-start(pred[4,8]{1,0:T(4,128)(4,1)S(1)} %broadcast_and_fusion) | copy-start | bytes 100
  125.4 5.0 collective-permute-start.5
  126.7 3.9 collective-permute-start.4
  130.3 31.5 %copy-start.21 = (pred[128]{0:T(512)(128)(4,1)}, pred[128]{0:T(512)(128)(4,1)S(1)}, u32[]{:S(2)}) copy-start(pred[128]{0:T(512)(128)(4,1)S(1)} %iota_compare_fusion.7) | copy-start | bytes 388
  132.1 29.7 %collective-permute-start.9 = (f32[1,4,8,128]{3,2,1,0:T(8,128)S(1)}, f32[1,4,8,128]{3,2,1,0:T(8,128)S(1)}, u32[]{:S(2)}, u32[]{:S(2)}) collective-permute-start(f32[1,4,8,128]{3,2,1,0:T(8,128)S(1)} %bitcast.140), channel_id=1, source_target_pairs={{1,0},{2,1},{3,2},{4,3},{5,4},{6,5},{7,6},{8,7},{9,8},{10,9},{11,1... | collective-permute-start | bytes 49160 | tf_op jit(solution)/shard_map/ppermute | solution.py:22
  159.8 8.3 %collective-permute-start.8 = (f32[1,4,8,128]{3,2,1,0:T(8,128)S(1)}, f32[1,4,8,128]{3,2,1,0:T(8,128)S(1)}, u32[]{:S(2)}, u32[]{:S(2)}) collective-permute-start(f32[1,4,8,128]{3,2,1,0:T(8,128)S(1)} %bitcast.141), channel_id=1, source_target_pairs={{0,1},{1,2},{2,3},{3,4},{4,5},{5,6},{6,7},{7,8},{8,9},{9,10},{10,1... | collective-permute-start | bytes 49160 | tf_op jit(solution)/shard_map/ppermute | solution.py:19
  168.1 11.8 %collective-permute-start.11 = (f32[1,12,4,128]{3,2,1,0:T(4,128)S(1)}, f32[1,12,4,128]{3,2,1,0:T(4,128)S(1)}, u32[]{:S(2)}, u32[]{:S(2)}) collective-permute-start(f32[1,12,4,128]{3,2,1,0:T(4,128)S(1)} %get-tuple-element.31), channel_id=1, source_target_pairs={{16,0},{32,16},{48,32},{64,48},{80,64},{96,80},{112,96},{128,112},... | collective-permute-start | bytes 73736 | tf_op jit(solution)/shard_map/ppermute | solution.py:22
  169.4 11.2 %collective-permute-start.10 = (f32[1,12,4,128]{3,2,1,0:T(4,128)S(1)}, f32[1,12,4,128]{3,2,1,0:T(4,128)S(1)}, u32[]{:S(2)}, u32[]{:S(2)}) collective-permute-start(f32[1,12,4,128]{3,2,1,0:T(4,128)S(1)} %get-tuple-element.30), channel_id=1, source_target_pairs={{0,16},{16,32},{32,48},{48,64},{64,80},{80,96},{96,112},{112,128},... | collective-permute-start | bytes 73736 | tf_op jit(solution)/shard_map/ppermute | solution.py:19
  181.3 11.6 %all-to-all-start.2 = ((f32[16,4,8,128]{3,2,1,0:T(8,128)}), f32[16,4,8,128]{3,2,1,0:T(8,128)}, u32[]{:S(2)}, u32[]{:S(2)}) async-start(f32[16,4,8,128]{3,2,1,0:T(8,128)} %stack.18), calls=%async_computation.2 | async-start | bytes 524288 | tf_op jit(solution)/shard_map/all_to_all | solution.py:137
  185.9 4.1 copy-start.6
  185.9 4.1 copy-start.7
  192.9 38.8 %copy-start.19 = (pred[4,8]{1,0:T(4,128)(4,1)S(1)}, pred[4,8]{1,0:T(4,128)(4,1)}, u32[]{:S(2)}) copy-start(pred[4,8]{1,0:T(4,128)(4,1)} %copy-done.18) | copy-start | bytes 100
  193.0 38.8 %copy-start.22 = (pred[128]{0:T(512)(128)(4,1)S(1)}, pred[128]{0:T(512)(128)(4,1)}, u32[]{:S(2)}) copy-start(pred[128]{0:T(512)(128)(4,1)} %copy-done.21) | copy-start | bytes 388
  222.6 38.5 %collective-permute-start.7 = (f32[4,64,4,128]{3,2,1,0:T(4,128)}, f32[4,64,4,128]{3,2,1,0:T(4,128)S(1)}, u32[]{:S(2)}, u32[]{:S(2)}) collective-permute-start(f32[4,64,4,128]{3,2,1,0:T(4,128)} %get-tuple-element.20), channel_id=1, source_target_pairs={{16,0},{32,16},{48,32},{64,48},{80,64},{96,80},{112,96},{128,112},... | collective-permute-start | bytes 1572872 | tf_op jit(solution)/shard_map/ppermute | solution.py:22
  223.9 37.3 %collective-permute-start.6 = (f32[4,64,4,128]{3,2,1,0:T(4,128)}, f32[4,64,4,128]{3,2,1,0:T(4,128)S(1)}, u32[]{:S(2)}, u32[]{:S(2)}) collective-permute-start(f32[4,64,4,128]{3,2,1,0:T(4,128)} %get-tuple-element.19), channel_id=1, source_target_pairs={{0,16},{16,32},{32,48},{48,64},{64,80},{80,96},{96,112},{112,128},... | collective-permute-start | bytes 1572872 | tf_op jit(solution)/shard_map/ppermute | solution.py:19
  233.3 16.7 %collective-permute-start.15 = (f32[1,4,8,128]{3,2,1,0:T(8,128)S(1)}, f32[1,4,8,128]{3,2,1,0:T(8,128)S(1)}, u32[]{:S(2)}, u32[]{:S(2)}) collective-permute-start(f32[1,4,8,128]{3,2,1,0:T(8,128)S(1)} %get-tuple-element.11), channel_id=1, source_target_pairs={{1,0},{2,1},{3,2},{4,3},{5,4},{6,5},{7,6},{8,7},{9,8},{10,9},{11,1... | collective-permute-start | bytes 49160 | tf_op jit(solution)/shard_map/ppermute | solution.py:22
  238.6 11.4 %collective-permute-start.14 = (f32[1,4,8,128]{3,2,1,0:T(8,128)S(1)}, f32[1,4,8,128]{3,2,1,0:T(8,128)S(1)}, u32[]{:S(2)}, u32[]{:S(2)}) collective-permute-start(f32[1,4,8,128]{3,2,1,0:T(8,128)S(1)} %get-tuple-element.11), channel_id=1, source_target_pairs={{0,1},{1,2},{2,3},{3,4},{4,5},{5,6},{6,7},{7,8},{8,9},{9,10},{10,1... | collective-permute-start | bytes 49160 | tf_op jit(solution)/shard_map/ppermute | solution.py:19
  241.3 28.8 %all-to-all-start.3 = ((f32[16,4,8,128]{3,2,1,0:T(8,128)}), f32[16,4,8,128]{3,2,1,0:T(8,128)}, u32[]{:S(2)}, u32[]{:S(2)}) async-start(f32[16,4,8,128]{3,2,1,0:T(8,128)} %stack.19), calls=%async_computation.3 | async-start | bytes 524288 | tf_op jit(solution)/shard_map/all_to_all | solution.py:137
  250.0 9.7 %copy-start.14 = (f32[1,4,8,128]{3,2,1,0:T(8,128)}, f32[1,4,8,128]{3,2,1,0:T(8,128)S(1)}, u32[]{:S(2)}) copy-start(f32[1,4,8,128]{3,2,1,0:T(8,128)S(1)} %collective-permute-done.15) | copy-start | bytes 49156
  250.0 9.7 %copy-start.15 = (f32[1,4,8,128]{3,2,1,0:T(8,128)}, f32[1,4,8,128]{3,2,1,0:T(8,128)S(1)}, u32[]{:S(2)}) copy-start(f32[1,4,8,128]{3,2,1,0:T(8,128)S(1)} %collective-permute-done.14) | copy-start | bytes 49156
  250.1 9.6 %collective-permute-start.17 = (f32[1,12,4,128]{3,2,1,0:T(4,128)S(1)}, f32[1,12,4,128]{3,2,1,0:T(4,128)S(1)}, u32[]{:S(2)}, u32[]{:S(2)}) collective-permute-start(f32[1,12,4,128]{3,2,1,0:T(4,128)S(1)} %get-tuple-element.29), channel_id=1, source_target_pairs={{16,0},{32,16},{48,32},{64,48},{80,64},{96,80},{112,96},{128,112},... | collective-permute-start | bytes 73736 | tf_op jit(solution)/shard_map/ppermute | solution.py:22
  251.4 9.0 %collective-permute-start.16 = (f32[1,12,4,128]{3,2,1,0:T(4,128)S(1)}, f32[1,12,4,128]{3,2,1,0:T(4,128)S(1)}, u32[]{:S(2)}, u32[]{:S(2)}) collective-permute-start(f32[1,12,4,128]{3,2,1,0:T(4,128)S(1)} %get-tuple-element.28), channel_id=1, source_target_pairs={{0,16},{16,32},{32,48},{48,64},{64,80},{80,96},{96,112},{112,128},... | collective-permute-start | bytes 73736 | tf_op jit(solution)/shard_map/ppermute | solution.py:19
  261.1 9.0 %copy-start.8 = (f32[4,64,4,128]{3,2,1,0:T(4,128)}, f32[4,64,4,128]{3,2,1,0:T(4,128)S(1)}, u32[]{:S(2)}) copy-start(f32[4,64,4,128]{3,2,1,0:T(4,128)S(1)} %collective-permute-done.7) | copy-start | bytes 1572868
  261.2 8.9 %copy-start.9 = (f32[4,64,4,128]{3,2,1,0:T(4,128)}, f32[4,64,4,128]{3,2,1,0:T(4,128)S(1)}, u32[]{:S(2)}) copy-start(f32[4,64,4,128]{3,2,1,0:T(4,128)S(1)} %collective-permute-done.6) | copy-start | bytes 1572868
  270.1 39.9 %copy-start.20 = (pred[4,8]{1,0:T(4,128)(4,1)S(1)}, pred[4,8]{1,0:T(4,128)(4,1)}, u32[]{:S(2)}) copy-start(pred[4,8]{1,0:T(4,128)(4,1)} %copy-done.18) | copy-start | bytes 100
  270.1 39.9 %copy-start.23 = (pred[128]{0:T(512)(128)(4,1)S(1)}, pred[128]{0:T(512)(128)(4,1)}, u32[]{:S(2)}) copy-start(pred[128]{0:T(512)(128)(4,1)} %copy-done.21) | copy-start | bytes 388
  299.4 48.0 %collective-permute-start.13 = (f32[4,64,4,128]{3,2,1,0:T(4,128)}, f32[4,64,4,128]{3,2,1,0:T(4,128)}, u32[]{:S(2)}, u32[]{:S(2)}) collective-permute-start(f32[4,64,4,128]{3,2,1,0:T(4,128)} %get-tuple-element.18), channel_id=1, source_target_pairs={{16,0},{32,16},{48,32},{64,48},{80,64},{96,80},{112,96},{128,112},... | collective-permute-start | bytes 1572872 | tf_op jit(solution)/shard_map/ppermute | solution.py:22
  300.7 46.7 %collective-permute-start.12 = (f32[4,64,4,128]{3,2,1,0:T(4,128)}, f32[4,64,4,128]{3,2,1,0:T(4,128)}, u32[]{:S(2)}, u32[]{:S(2)}) collective-permute-start(f32[4,64,4,128]{3,2,1,0:T(4,128)} %get-tuple-element.17), channel_id=1, source_target_pairs={{0,16},{16,32},{32,48},{48,64},{64,80},{80,96},{96,112},{112,128},... | collective-permute-start | bytes 1572872 | tf_op jit(solution)/shard_map/ppermute | solution.py:19
  312.2 21.6 %collective-permute-start.21 = (f32[1,4,8,128]{3,2,1,0:T(8,128)S(1)}, f32[1,4,8,128]{3,2,1,0:T(8,128)S(1)}, u32[]{:S(2)}, u32[]{:S(2)}) collective-permute-start(f32[1,4,8,128]{3,2,1,0:T(8,128)S(1)} %get-tuple-element.9), channel_id=1, source_target_pairs={{1,0},{2,1},{3,2},{4,3},{5,4},{6,5},{7,6},{8,7},{9,8},{10,9},{11,1... | collective-permute-start | bytes 49160 | tf_op jit(solution)/shard_map/ppermute | solution.py:22
  322.4 11.3 %collective-permute-start.20 = (f32[1,4,8,128]{3,2,1,0:T(8,128)S(1)}, f32[1,4,8,128]{3,2,1,0:T(8,128)S(1)}, u32[]{:S(2)}, u32[]{:S(2)}) collective-permute-start(f32[1,4,8,128]{3,2,1,0:T(8,128)S(1)} %get-tuple-element.9), channel_id=1, source_target_pairs={{0,1},{1,2},{2,3},{3,4},{4,5},{5,6},{6,7},{7,8},{8,9},{9,10},{10,1... | collective-permute-start | bytes 49160 | tf_op jit(solution)/shard_map/ppermute | solution.py:19
  325.1 27.5 %all-to-all-start.4 = ((f32[16,4,8,128]{3,2,1,0:T(8,128)}), f32[16,4,8,128]{3,2,1,0:T(8,128)}, u32[]{:S(2)}, u32[]{:S(2)}) async-start(f32[16,4,8,128]{3,2,1,0:T(8,128)} %stack.20), calls=%async_computation.4 | async-start | bytes 524288 | tf_op jit(solution)/shard_map/all_to_all | solution.py:137
  333.8 12.8 %collective-permute-start.23 = (f32[1,12,4,128]{3,2,1,0:T(4,128)S(1)}, f32[1,12,4,128]{3,2,1,0:T(4,128)S(1)}, u32[]{:S(2)}, u32[]{:S(2)}) collective-permute-start(f32[1,12,4,128]{3,2,1,0:T(4,128)S(1)} %get-tuple-element.27), channel_id=1, source_target_pairs={{16,0},{32,16},{48,32},{64,48},{80,64},{96,80},{112,96},{128,112},... | collective-permute-start | bytes 73736 | tf_op jit(solution)/shard_map/ppermute | solution.py:22
  335.1 12.3 %collective-permute-start.22 = (f32[1,12,4,128]{3,2,1,0:T(4,128)S(1)}, f32[1,12,4,128]{3,2,1,0:T(4,128)S(1)}, u32[]{:S(2)}, u32[]{:S(2)}) collective-permute-start(f32[1,12,4,128]{3,2,1,0:T(4,128)S(1)} %get-tuple-element.26), channel_id=1, source_target_pairs={{0,16},{16,32},{32,48},{48,64},{64,80},{80,96},{96,112},{112,128},... | collective-permute-start | bytes 73736 | tf_op jit(solution)/shard_map/ppermute | solution.py:19
  352.6 50.8 %copy-start.24 = (s32[256]{0:T(256)S(1)}, s32[256]{0:T(256)}, u32[]{:S(2)}) copy-start(s32[256]{0:T(256)} %param.29) | copy-start | bytes 3076
  352.6 50.8 %copy-start.25 = (s32[256]{0:T(256)S(1)}, s32[256]{0:T(256)}, u32[]{:S(2)}) copy-start(s32[256]{0:T(256)} %param.28) | copy-start | bytes 3076
  352.6 50.8 %copy-start.26 = (s32[256]{0:T(256)S(1)}, s32[256]{0:T(256)}, u32[]{:S(2)}) copy-start(s32[256]{0:T(256)} %param.27) | copy-start | bytes 3076
  380.6 1.0 copy-start.2
  382.7 103.6 %collective-permute-start.19 = (f32[4,64,4,128]{3,2,1,0:T(4,128)}, f32[4,64,4,128]{3,2,1,0:T(4,128)}, u32[]{:S(2)}, u32[]{:S(2)}) collective-permute-start(f32[4,64,4,128]{3,2,1,0:T(4,128)} %get-tuple-element.16), channel_id=1, source_target_pairs={{16,0},{32,16},{48,32},{64,48},{80,64},{96,80},{112,96},{128,112},... | collective-permute-start | bytes 1572872 | tf_op jit(solution)/shard_map/ppermute | solution.py:22
  384.0 102.4 %collective-permute-start.18 = (f32[4,64,4,128]{3,2,1,0:T(4,128)}, f32[4,64,4,128]{3,2,1,0:T(4,128)}, u32[]{:S(2)}, u32[]{:S(2)}) collective-permute-start(f32[4,64,4,128]{3,2,1,0:T(4,128)} %get-tuple-element.15), channel_id=1, source_target_pairs={{0,16},{16,32},{32,48},{48,64},{64,80},{80,96},{96,112},{112,128},... | collective-permute-start | bytes 1572872 | tf_op jit(solution)/shard_map/ppermute | solution.py:19
  394.7 96.8 %all-to-all-start.5 = ((f32[16,4,8,128]{3,2,1,0:T(8,128)}), f32[16,4,8,128]{3,2,1,0:T(8,128)}, u32[]{:S(2)}, u32[]{:S(2)}) async-start(f32[16,4,8,128]{3,2,1,0:T(8,128)} %stack.21), calls=%async_computation.5 | async-start | bytes 524288 | tf_op jit(solution)/shard_map/all_to_all | solution.py:137
  430.7 27.9 %copy-start.3 = (f32[4,64,8,128]{3,2,1,0:T(8,128)S(1)}, f32[4,64,8,128]{3,2,1,0:T(8,128)}, u32[]{:S(2)}) copy-start(f32[4,64,8,128]{3,2,1,0:T(8,128)} %copy-done.2) | copy-start | bytes 3145732
  520.5 28.2 %copy-start.11 = (f32[256,4]{1,0:T(8,128)S(1)}, f32[256,4]{1,0:T(8,128)}, u32[]{:S(2)}) copy-start(f32[256,4]{1,0:T(8,128)} %gather_fusion.1) | copy-start | bytes 12292
  520.5 28.2 %copy-start.12 = (f32[256,4]{1,0:T(8,128)S(1)}, f32[256,4]{1,0:T(8,128)}, u32[]{:S(2)}) copy-start(f32[256,4]{1,0:T(8,128)} %gather_fusion.2) | copy-start | bytes 12292
  520.5 200.4 %copy-start.1 = (bf16[4,32,32,128]{3,2,1,0:T(8,128)(2,1)S(1)}, bf16[4,32,32,128]{3,2,1,0:T(8,128)(2,1)}, u32[]{:S(2)}) copy-start(bf16[4,32,32,128]{3,2,1,0:T(8,128)(2,1)} %param.22) | copy-start | bytes 3145732
